TPU v7x, 512 devices: a whole 4x8x8 slice. The times are simulated.
512 devices in a mesh: walk: 32 (over z_hi, y, core), slab: 16 (over x, z_lo).
Axes of the slice: x: 4, y: 8, z: 8 (z_hi: 2, z_lo: 4; z = z_hi * 4 + z_lo), core: 2. Of those that a mesh axis runs over, the one named last changes fastest.
Arguments:
- ci_blocks: float32 [2, 3072, 4096], P(None, 'walk', 'slab'), may hold values from -6 to 6
- integrals: float32 [2, 4096, 4096], P(None, 'slab', 'walk'), as said below
- live_counts: int32 [32], P('walk'), may hold values from 24 to 96, as said below
- walk_kind: int32 [3072], P('walk'), may hold values from 0 to 2
- walk_sign: int32 [3072], P('walk'), may hold values from 0 to 1
Outputs:
- first_sigma: float32 [2, 3072, 4096], P(None, 'walk', 'slab')
- second_sigma: float32 [2, 3072, 4096], P(None, 'walk', 'slab')
Inputs may be any that keep to these rules, and one draw needn't show every extreme that they name: integrals[k] is exactly symmetric for each k, every entry of magnitude under 9 / sqrt(4096). `live_counts`: some walk index has all 96 slots live in every draw.
All inputs are finite; a program needn't handle non-finite values.
Results may differ from a plain program's by a relative error of at most 0.000075.
Values sent between devices are 32-bit elements; how exact they have to be, the bound alone decides.
A program may use at most 64 MiB of HBM per device.

v0:
```python
import jax
import jax.numpy as jnp
from jax import lax
from jax.sharding import PartitionSpec as P


def on_device(ci_blocks, integrals, live_counts, walk_kind, walk_sign):
    rows = lax.all_gather(integrals, "walk", axis=2, tiled=True)
    slots = ci_blocks.shape[1]
    position = jnp.arange(slots, dtype=jnp.int32)
    live = position < live_counts[0]
    plus_on = jnp.where(live & (walk_kind != 1), 1.0, 0.0).astype(jnp.float32)
    minus_on = jnp.where(live & (walk_kind != 0), 1.0, 0.0).astype(jnp.float32)
    minus_on = minus_on * (2 * walk_sign - 1).astype(jnp.float32)
    scale = jnp.stack([plus_on, minus_on])[:, :, None]

    def add_columns(piece):
        return jnp.einsum("kwn,kpn->kwp", piece, rows, precision=lax.Precision.HIGHEST)

    first = scale * add_columns(lax.all_gather(ci_blocks, "slab", axis=2, tiled=True))
    second = scale * add_columns(lax.all_gather(first, "slab", axis=2, tiled=True))
    return (first, second)


def solution(mesh):
    placed = (P(None, "walk", "slab"), P(None, "slab", "walk"), P("walk"), P("walk"), P("walk"))
    return jax.shard_map(
        on_device,
        mesh=mesh,
        in_specs=placed,
        out_specs=(P(None, "walk", "slab"), P(None, "walk", "slab")),
        check_vma=False,
    )
```

profile of v0, /device:TPU:6, one launch (start us, length us, event | category | flops | bytes accessed | tf_op | source)
XLA Modules:
  0.0 369.9 jit_solution(702352706293899418)
XLA Ops:
  7.2 0.0 all-gather.4.cloned.1.call-start
  7.2 0.7 all-gather.4.cloned.1.call-update
  7.9 0.0 all-gather.6.cloned.1.call-start
  7.9 0.7 all-gather.6.cloned.1.call-update
  8.6 0.0 all-gather.8.cloned.1.call-start
  9.3 0.7 fusion.1
  10.0 95.1 %all-gather.4.cloned.1.call-done = f32[2,96,4096]{2,1,0:T(8,128)} async-done(((f32[2,96,256]{2,1,0:T(8,128)}), f32[2,96,4096]{2,1,0:T(8,128)}) %all-gather.4.cloned.1.call-update) | async-done | bytes 3145744 | tf_op jit(solution)/shard_map/all_gather | solution.py:20
  105.1 148.2 %all-gather.6.cloned.1.call-done = f32[2,256,4096]{2,1,0:T(8,128)} async-done(((f32[2,256,128]{2,1,0:T(8,128)}), f32[2,256,4096]{2,1,0:T(8,128)}) %all-gather.6.cloned.1.call-update) | async-done | bytes 8388624 | tf_op jit(solution)/shard_map/all_gather | solution.py:8
  253.4 12.8 %convolution_multiply_fusion.1 = f32[2,96,256]{2,1,0:T(8,128)} fusion(f32[2,96,4096]{2,1,0:T(8,128)} %all-gather.4.cloned.1.call-done, f32[2,256,4096]{2,1,0:T(8,128)} %all-gather.6.cloned.1.call-done, f32[2,96]{1,0:T(2,128)S(1)} %pad_maximum_fusion), kind=kOutput, calls=%fused_computation.1 | convolution fusion | flops 2415968256 | bytes 11731712 | tf_op jit(solution)/shard_map/kwn,kpn->kwp/dot_general | solution.py:18
  266.2 0.0 all-gather.8.cloned.1.call-update
  266.2 84.4 %all-gather.8.cloned.1.call-done = f32[2,96,4096]{2,1,0:T(8,128)} async-done(((f32[2,96,256]{2,1,0:T(8,128)}), f32[2,96,4096]{2,1,0:T(8,128)}) %all-gather.8.cloned.1.call-update) | async-done | bytes 3145744 | tf_op jit(solution)/shard_map/all_gather | solution.py:21
  350.6 12.8 %convolution_multiply_fusion = f32[2,96,256]{2,1,0:T(8,128)} fusion(f32[2,96,4096]{2,1,0:T(8,128)} %all-gather.8.cloned.1.call-done, f32[2,256,4096]{2,1,0:T(8,128)} %all-gather.6.cloned.1.call-done, f32[2,96]{1,0:T(2,128)S(1)} %pad_maximum_fusion), kind=kOutput, calls=%fused_computation | convolution fusion | flops 2415968256 | bytes 11731712 | tf_op jit(solution)/shard_map/kwn,kpn->kwp/dot_general | solution.py:18
  (1 shorter events, 0.0 us)
Async XLA Ops:
  7.2 98.0 %all-gather.4.cloned.1.call-start = ((), (), s32[]{:S(2)}) async-start(), calls=%async_computation | async-start | bytes 3342336 | tf_op jit(solution)/shard_map/all_gather | solution.py:20
  7.9 245.5 %all-gather.6.cloned.1.call-start = ((), (), s32[]{:S(2)}) async-start(), calls=%async_computation.1 | async-start | bytes 8650752 | tf_op jit(solution)/shard_map/all_gather | solution.py:8
  8.6 341.9 %all-gather.8.cloned.1.call-start = ((), (), s32[]{:S(2)}) async-start(), calls=%async_computation.2 | async-start | bytes 3342336 | tf_op jit(solution)/shard_map/all_gather | solution.py:21
Sparse Core Ops, SparseCore 0:
  10.1 95.0 all-gather.3
  108.3 145.0 all-gather.5
  266.4 84.1 all-gather.7
where the time goes:
time: 376 us; the launch traced here: 370 us
  waiting for transfers between devices  329 us (88%)
  matrix products  25.6 us (7%)
  between operations  14.4 us (4%)
    all_gather x1, waiting for transfers between devices, on_device(): rows = lax.all_gather(integrals, 'walk', axis=2, tiled=True)  148 us
    all_gather x1, waiting for transfers between devices, on_device(): lax.all_gather(ci_blocks, 'slab', axis=2, tiled=True)  95.1 us
    all_gather x1, waiting for transfers between devices, on_device(): lax.all_gather(first, 'slab', axis=2, tiled=True)  84.4 us
    dot_general x2, matrix products, add_columns(): jnp.einsum('kwn,kpn->kwp', piece, rows, precision=lax.Precision.HIGHEST)  25.6 us
  transfers between devices with their start and end apart: 3, of which 3 were waited for; matrix products, arithmetic and copies ran while one was open for 0% of the time, Pallas kernels for 0%

commit v1 on v0

v1 whole, which is shorter than its diff:
```python
import functools

import jax
import jax.numpy as jnp
from jax import lax
from jax.experimental import pallas as pl
from jax.experimental.pallas import tpu as pltpu
from jax.sharding import PartitionSpec as P

MESH = pl.DeviceIdType.MESH
F32 = jnp.float32
BF16 = jnp.bfloat16


def device(x, y, z, c):
    return ((z // 4) * 16 + y * 2 + c, x * 4 + z % 4)


def split(a):
    high = a.astype(BF16)
    return high, (a - high.astype(F32)).astype(BF16)


def product(a, b, dims):
    dot = functools.partial(lax.dot_general, dimension_numbers=(dims, ((), ())), preferred_element_type=F32)
    return dot(a[0], b[0]) + (dot(a[0], b[1]) + dot(a[1], b[0]))


def kernel(
    ci, integrals, live, kind, sign, first_out, second_out,
    scaled, turned, cbuf, gbuf, part, parts_in, firsts, fold, fold_in, sums, sums_in, swap_in,
    g_send, g_recv, c_send, c_recv, mate_send, mate_recv, y_send, y_recv,
    rs_send, rs_recv, ag_send, ag_recv, fo_send, fo_recv, z_send, z_recv, sw_send, sw_recv,
):
    walk, slab = lax.axis_index("walk"), lax.axis_index("slab")
    x, zl = slab // 4, slab % 4
    zh, y, c = walk // 16, (walk // 2) % 8, walk % 2
    z = zh * 4 + zl

    def remote(src, dst, send, recv, to):
        return pltpu.make_async_remote_copy(
            src_ref=src, dst_ref=dst, send_sem=send, recv_sem=recv, device_id=to, device_id_type=MESH
        )

    def giver(quarter, k):
        return (2 * zh + c, y, (x // 2) * 4 + quarter, k)

    def is_me(place):
        return (place[0] == x) & (place[1] == y) & (place[2] == z) & (place[3] == c)

    barrier = pltpu.get_barrier_semaphore()
    near = [(x, y, (z + dz) % 8, (c + dc) % 2) for dz in range(8) for dc in range(2) if dz or dc]
    near += [(x, (y + 1) % 8, z, c), (x, (y + 7) % 8, z, c)]
    near += [((x + d) % 4, y, z, c) for d in (1, 2, 3)]
    for place in near:
        pl.semaphore_signal(barrier, inc=1, device_id=device(*place), device_id_type=MESH)
    for quarter in range(4):
        for k in range(2):
            place = giver(quarter, k)

            @pl.when(jnp.logical_not(is_me(place)))
            def _():
                pl.semaphore_signal(barrier, inc=1, device_id=device(*place), device_id_type=MESH)

    def taker(yy):
        return (2 * zh + yy // 4, y, (x // 2) * 4 + yy % 4, x % 2)

    mine = [is_me(taker(yy)) for yy in range(8)]
    own = functools.reduce(lambda a, b: a + b, [m.astype(jnp.int32) for m in mine])

    rows = lax.broadcasted_iota(jnp.int32, (96, 96), 0)
    cols = lax.broadcasted_iota(jnp.int32, (96, 96), 1)

    def column(line):
        return jnp.sum(jnp.where(rows == cols, jnp.broadcast_to(line, (96, 96)), 0.0), axis=1, keepdims=True)

    position = lax.broadcasted_iota(jnp.int32, (1, 96), 1)
    alive = position < live[...]
    plus = jnp.where(alive & (kind[...] != 1), 1.0, 0.0).astype(F32)
    minus = jnp.where(alive & (kind[...] != 0), 1.0, 0.0).astype(F32) * (2 * sign[...] - 1).astype(F32)
    scale = [column(plus), column(minus)]
    for k in range(2):
        scaled[k] = ci[k] * scale[k]
        turned[k] = integrals[k].T
    cbuf[zl, zh * 2 + c] = scaled[c]

    pl.semaphore_wait(barrier, len(near) + 8 - own)

    for e in range(2):
        for k in range(2):
            quarter = 2 * c + e
            to = (x, y, zh * 4 + quarter, k)
            src = turned.at[k, pl.ds(e * 64, 64)]
            here = is_me(to)

            @pl.when(here)
            def _():
                gbuf[zl, y] = src[...]

            @pl.when(jnp.logical_not(here))
            def _():
                remote(src, gbuf.at[zl, y], g_send.at[e, k], g_recv.at[zl], device(*to)).start()

    mate = device(x, y, z, 1 - c)
    slot = cbuf.at[zl, zh * 2 + c]
    mate_copy = remote(scaled.at[1 - c], slot, mate_send.at[0], mate_recv.at[0], mate)
    mate_copy.start()
    sent = []

    def z_step(way):
        return (z + (1 if way == 0 else 7)) % 8

    def y_step(way):
        return (y + (1 if way == 0 else 7)) % 8

    for dk in range(2):
        k = (c + dk) % 2
        for way in range(2):
            copy = remote(scaled.at[k], slot, c_send.at[way, 0, dk], c_recv.at[way, 0, dk], device(x, y, z_step(way), k))
            copy.start()
            sent.append(copy)

    def c_block(way, d, dk):
        source = (z + (8 - d if way == 0 else d)) % 8
        return cbuf.at[source % 4, (source // 4) * 2 + (c + dk) % 2]

    def y_block(way, d, rz):
        source = (y + (8 - d if way == 0 else d)) % 8
        return gbuf.at[(zl + 4 - rz) % 4, source]

    def c_copy(way, d, dk):
        block = c_block(way, d - 1, dk)
        return remote(block, block, c_send.at[way, d - 1, dk], c_recv.at[way, d - 1, dk], device(x, y, z_step(way), c))

    def c_wait(way, d, dk):
        block = c_block(way, d, dk)
        remote(block, block, c_send.at[way, d - 1, dk], c_recv.at[way, d - 1, dk], mate).wait_recv()

    def y_copy(way, d, rz):
        block = y_block(way, d - 1, rz)
        return remote(block, block, y_send.at[way, d - 1, rz], y_recv.at[way, d - 1, rz], device(x, y_step(way), z, c))

    def y_wait(way, d, rz):
        block = y_block(way, d, rz)
        remote(block, block, y_send.at[way, d - 1, rz], y_recv.at[way, d - 1, rz], mate).wait_recv()

    for rz in range(4):
        source = (zl + 4 - rz) % 4
        block = gbuf.at[source, y]
        arrived = remote(block, block, g_send.at[0, 0], g_recv.at[source], mate)
        if rz == 0:

            @pl.when(c != zl // 2)
            def _():
                arrived.wait_recv()
        else:
            arrived.wait_recv()
        for way in range(2):
            copy = y_copy(way, 1, rz)
            copy.start()
            sent.append(copy)

    for d in range(2, 5):
        for dk in range(2):
            for way in range(2):
                c_wait(way, d - 1, dk)
                if d < 4 or way == dk:
                    copy = c_copy(way, d, dk)
                    copy.start()
                    sent.append(copy)
        for rz in range(4):
            for way in range(2):
                y_wait(way, d - 1, rz)
                if d < 4 or way == rz // 2:
                    copy = y_copy(way, d, rz)
                    copy.start()
                    sent.append(copy)
    for way in range(2):
        c_wait(way, 4, way)
    mate_block = cbuf.at[zl, zh * 2 + 1 - c]
    remote(mate_block, mate_block, mate_send.at[0], mate_recv.at[0], mate).wait_recv()
    for rz in range(4):
        y_wait(rz // 2, 4, rz)

    total = None
    for s in range(4):
        a = split(cbuf[s].reshape(384, 256))
        b = split(gbuf[s].reshape(512, 256))
        one = product(a, b, ((1,), (1,)))
        total = one if total is None else total + one
    part[...] = total.reshape(4, 96, 512)

    for d in range(1, 4):
        to = (x + d) % 4
        copy = remote(part.at[to], parts_in.at[d - 1], rs_send.at[d - 1], rs_recv.at[d - 1], device(to, y, z, c))
        copy.start()
        sent.append(copy)
    for d in range(1, 4):
        remote(part.at[0], parts_in.at[d - 1], rs_send.at[d - 1], rs_recv.at[d - 1], mate).wait_recv()
    firsts[x] = (part[x] + parts_in[0]) + (parts_in[1] + parts_in[2])
    for d in range(1, 4):
        copy = remote(firsts.at[x], firsts.at[x], ag_send.at[d - 1], ag_recv.at[d - 1], device((x + d) % 4, y, z, c))
        copy.start()
        sent.append(copy)

    lane = lax.broadcasted_iota(jnp.int32, (48, 128), 1)
    for t in range(4):
        tile = firsts[x, :, pl.ds(t * 128, 128)]
        top, low = tile[:48], tile[48:]
        fold[2 * t] = jnp.where(lane < 64, top, pltpu.roll(low, 64, 1))
        fold[2 * t + 1] = jnp.where(lane < 64, pltpu.roll(top, 64, 1), low)
    for yy in range(8):

        @pl.when(mine[yy])
        def _():
            fold_in[c, zl] = fold[yy]

        @pl.when(jnp.logical_not(mine[yy]))
        def _():
            remote(fold.at[yy], fold_in.at[c, zl], fo_send.at[yy], fo_recv.at[c, zl], device(*taker(yy))).start()

    for d in range(1, 4):
        block = firsts.at[(x + 4 - d) % 4]
        remote(block, block, ag_send.at[d - 1], ag_recv.at[d - 1], mate).wait_recv()

    def second_part(target):
        a = split(firsts[pl.ds((target // 4) * 2, 2)].reshape(192, 512))
        b = split(gbuf[target % 4].reshape(512, 256))
        sums[target] = product(a, b, ((1,), (0,))).reshape(2, 96, 256)

    def target_of(way, d):
        return (z + (d if way == 0 else 8 - d)) % 8

    def z_copy(way, d, h):
        return remote(
            sums.at[target_of(way, d), h], sums_in.at[way, d - 1, h],
            z_send.at[way, d - 1, h], z_recv.at[way, d - 1, h], device(x, y, z_step(way), c),
        )

    def z_start(way, d, h):
        copy = z_copy(way, d, h)
        copy.start()
        sent.append(copy)

    def z_add(way, d, h):
        z_copy(way, d, h).wait_recv()
        target = target_of(way, d - 1)
        sums[target, h] = sums[target, h] + sums_in[way, d - 1, h]

    second_part(target_of(0, 4))
    z_start(0, 4, 0)
    z_start(1, 4, 1)
    for way in range(2):
        second_part(target_of(way, 3))
        z_start(way, 3, 1 - way)
    for d in (2, 1):
        for way in range(2):
            second_part(target_of(way, d))
    second_part(z)
    for way in range(2):
        z_add(way, 4, way)
        z_start(way, 3, way)
    for d in (3, 2):
        for half in range(2):
            for way in range(2):
                h = 1 - way if half == 0 else way
                z_add(way, d, h)
                z_start(way, d - 1, h)
    for half in range(2):
        for way in range(2):
            z_add(way, 1, 1 - way if half == 0 else way)

    copy = remote(sums.at[z, 1 - c], swap_in.at[0], sw_send.at[0], sw_recv.at[0], mate)
    copy.start()
    sent.append(copy)

    for k in range(2):
        for quarter in range(4):
            block = fold_in.at[k, quarter]

            @pl.when(jnp.logical_not(is_me(giver(quarter, k))))
            def _():
                remote(block, block, fo_send.at[0], fo_recv.at[k, quarter], mate).wait_recv()

        for t in range(2):
            left, right = fold_in[k, 2 * t], fold_in[k, 2 * t + 1]
            first_out[k, :48, t * 128 : t * 128 + 128] = jnp.where(lane < 64, left, pltpu.roll(right, 64, 1))
            first_out[k, 48:, t * 128 : t * 128 + 128] = jnp.where(lane < 64, pltpu.roll(left, 64, 1), right)

    scale_mine = jnp.where(c == 0, scale[0], scale[1])
    scale_other = jnp.where(c == 0, scale[1], scale[0])
    second_out[c] = sums[z, c] * scale_mine
    copy.wait_recv()
    second_out[1 - c] = swap_in[0] * scale_other

    for copy in sent:
        copy.wait_send()
    mate_copy.wait_send()
    for e in range(2):
        for k in range(2):

            @pl.when(jnp.logical_not(is_me((x, y, zh * 4 + 2 * c + e, k))))
            def _():
                remote(turned.at[k, pl.ds(e * 64, 64)], gbuf.at[zl, y], g_send.at[e, k], g_recv.at[0], mate).wait_send()

    for yy in range(8):

        @pl.when(jnp.logical_not(mine[yy]))
        def _():
            remote(fold.at[yy], fold_in.at[0, 0], fo_send.at[yy], fo_recv.at[0, 0], mate).wait_send()


def on_device(ci_blocks, integrals, live_counts, walk_kind, walk_sign):
    vmem = pl.BlockSpec(memory_space=pltpu.VMEM)
    dma = pltpu.SemaphoreType.DMA
    shape = jax.ShapeDtypeStruct((2, 96, 256), F32)
    return pl.pallas_call(
        kernel,
        out_shape=(shape, shape),
        in_specs=[vmem] * 5,
        out_specs=(vmem, vmem),
        scratch_shapes=[
            pltpu.VMEM((2, 96, 256), F32),
            pltpu.VMEM((2, 128, 256), F32),
            pltpu.VMEM((4, 4, 96, 256), F32),
            pltpu.VMEM((4, 8, 64, 256), F32),
            pltpu.VMEM((4, 96, 512), F32),
            pltpu.VMEM((3, 96, 512), F32),
            pltpu.VMEM((4, 96, 512), F32),
            pltpu.VMEM((8, 48, 128), F32),
            pltpu.VMEM((2, 4, 48, 128), F32),
            pltpu.VMEM((8, 2, 96, 256), F32),
            pltpu.VMEM((2, 4, 2, 96, 256), F32),
            pltpu.VMEM((1, 96, 256), F32),
            dma((2, 2)), dma((4,)),
            dma((2, 4, 2)), dma((2, 4, 2)),
            dma((1,)), dma((1,)),
            dma((2, 4, 4)), dma((2, 4, 4)),
            dma((3,)), dma((3,)),
            dma((3,)), dma((3,)),
            dma((8,)), dma((2, 4)),
            dma((2, 4, 2)), dma((2, 4, 2)),
            dma((1,)), dma((1,)),
        ],
        compiler_params=pltpu.CompilerParams(
            collective_id=0, has_side_effects=True, vmem_limit_bytes=40 << 20
        ),
        name="sigma",
    )(
        ci_blocks, integrals, live_counts.reshape(1, 1),
        walk_kind.reshape(1, 96), walk_sign.reshape(1, 96),
    )


def solution(mesh):
    placed = (P(None, "walk", "slab"), P(None, "slab", "walk"), P("walk"), P("walk"), P("walk"))
    return jax.shard_map(
        on_device,
        mesh=mesh,
        in_specs=placed,
        out_specs=(P(None, "walk", "slab"), P(None, "walk", "slab")),
        check_vma=False,
    )
```

time: 376 us -> 95.6 us (0.25)
  the two profiles are of different devices: /device:TPU:6 before, /device:TPU:1 now
where the time goes in v1:
time: 95.6 us; the launch traced here: 95.4 us
  Pallas kernels  90.3 us (94%)
  local copies, waits for them, and re-layouts  3.89 us (4%)
  between operations  1.3 us (1%)
    pallas_call x1, Pallas kernels, on_device(): pl.pallas_call(kernel, out_shape=(shape, shape), in_specs=[vmem] * 5, out...  90.3 us
    unnamed x10, local copies, waits for them, and re-layouts  3.89 us

profile of v1, /device:TPU:1, one launch (start us, length us, event | category | flops | bytes accessed | tf_op | source)
XLA Modules:
  0.0 95.4 jit_solution(8994798564586997683)
XLA Ops:
  1.3 0.0 copy-start.2
  1.3 0.0 copy-start.3
  1.3 0.6 copy-done.2
  1.9 0.0 copy-done.3
  1.9 0.0 copy-start
  2.0 0.9 copy-done
  2.9 0.0 copy-start.1
  2.9 0.9 copy-done.1
  3.8 90.3 %sigma.1 = (f32[2,96,256]{2,1,0:T(8,128)S(1)}, f32[2,96,256]{2,1,0:T(8,128)S(1)}) custom-call(f32[2,96,256]{2,1,0:T(8,128)S(1)} %copy-done.1, f32[2,256,128]{2,1,0:T(8,128)S(1)} %copy-done, s32[1,1]{1,0:T(1,128)} %bitcast.3.live, s32[1,96]{1,0:T(1,128)S(1)} %bitcast.4, s32[1,96]{1,0:T(1,128)S(1)} %bitcast.5), custom_call_target="tpu_custom_call" | custom-call | tf_op jit(solution)/shard_map/sigma/pallas_call | solution.py:317
  94.1 0.7 copy.10
  94.8 0.7 copy.11
Async XLA Ops:
  1.3 0.7 copy-start.2
  1.3 0.7 copy-start.3
  1.9 0.9 copy-start
  2.9 0.9 copy-start.1

commit v2 on v1

--- a/solution.py
+++ b/solution.py
@@ -26,12 +26,24 @@
     return dot(a[0], b[0]) + (dot(a[0], b[1]) + dot(a[1], b[0]))
 
 
+OFFSETS = (0, -1, 1, -2, 2, -3, 3, 4)
+CHUNKS = ((0, 4), (4, 6), (6, 8))
+
+
 def kernel(
-    ci, integrals, live, kind, sign, first_out, second_out,
-    scaled, turned, cbuf, gbuf, part, parts_in, firsts, fold, fold_in, sums, sums_in, swap_in,
+    ci_hbm, integrals_hbm, live_hbm, kind_hbm, sign_hbm, first_out, second_out,
+    ci, integrals, live, kind, sign, in_sem, scaled, turned, cbuf, gbuf, part, parts_in, firsts, fold, fold_in, sums, sums_in, swap_in,
     g_send, g_recv, c_send, c_recv, mate_send, mate_recv, y_send, y_recv,
     rs_send, rs_recv, ag_send, ag_recv, fo_send, fo_recv, z_send, z_recv, sw_send, sw_recv,
 ):
+    loads = [
+        pltpu.make_async_copy(src, dst, in_sem.at[i])
+        for i, (src, dst) in enumerate(
+            zip((integrals_hbm, ci_hbm, live_hbm, kind_hbm, sign_hbm), (integrals, ci, live, kind, sign))
+        )
+    ]
+    for load in loads:
+        load.start()
     walk, slab = lax.axis_index("walk"), lax.axis_index("slab")
     x, zl = slab // 4, slab % 4
     zh, y, c = walk // 16, (walk // 2) % 8, walk % 2
@@ -62,10 +74,11 @@
             def _():
                 pl.semaphore_signal(barrier, inc=1, device_id=device(*place), device_id_type=MESH)
 
-    def taker(yy):
+    def taker(slot):
+        yy = (y + OFFSETS[slot] + 8) % 8
         return (2 * zh + yy // 4, y, (x // 2) * 4 + yy % 4, x % 2)
 
-    mine = [is_me(taker(yy)) for yy in range(8)]
+    mine = [is_me(taker(slot)) for slot in range(8)]
     own = functools.reduce(lambda a, b: a + b, [m.astype(jnp.int32) for m in mine])
 
     rows = lax.broadcasted_iota(jnp.int32, (96, 96), 0)
@@ -74,6 +87,8 @@
     def column(line):
         return jnp.sum(jnp.where(rows == cols, jnp.broadcast_to(line, (96, 96)), 0.0), axis=1, keepdims=True)
 
+    for load in loads:
+        load.wait()
     position = lax.broadcasted_iota(jnp.int32, (1, 96), 1)
     alive = position < live[...]
     plus = jnp.where(alive & (kind[...] != 1), 1.0, 0.0).astype(F32)
@@ -95,11 +110,11 @@
 
             @pl.when(here)
             def _():
-                gbuf[zl, y] = src[...]
+                gbuf[zl, 0] = src[...]
 
             @pl.when(jnp.logical_not(here))
             def _():
-                remote(src, gbuf.at[zl, y], g_send.at[e, k], g_recv.at[zl], device(*to)).start()
+                remote(src, gbuf.at[zl, 0], g_send.at[e, k], g_recv.at[zl], device(*to)).start()
 
     mate = device(x, y, z, 1 - c)
     slot = cbuf.at[zl, zh * 2 + c]
@@ -125,8 +140,8 @@
         return cbuf.at[source % 4, (source // 4) * 2 + (c + dk) % 2]
 
     def y_block(way, d, rz):
-        source = (y + (8 - d if way == 0 else d)) % 8
-        return gbuf.at[(zl + 4 - rz) % 4, source]
+        slot = min(2 * d - 1 + way, 7) if d else 0
+        return gbuf.at[(zl + 4 - rz) % 4, slot]
 
     def c_copy(way, d, dk):
         block = c_block(way, d - 1, dk)
@@ -137,8 +152,7 @@
         remote(block, block, c_send.at[way, d - 1, dk], c_recv.at[way, d - 1, dk], mate).wait_recv()
 
     def y_copy(way, d, rz):
-        block = y_block(way, d - 1, rz)
-        return remote(block, block, y_send.at[way, d - 1, rz], y_recv.at[way, d - 1, rz], device(x, y_step(way), z, c))
+        return remote(y_block(way, d - 1, rz), y_block(way, d, rz), y_send.at[way, d - 1, rz], y_recv.at[way, d - 1, rz], device(x, y_step(way), z, c))
 
     def y_wait(way, d, rz):
         block = y_block(way, d, rz)
@@ -146,7 +160,7 @@
 
     for rz in range(4):
         source = (zl + 4 - rz) % 4
-        block = gbuf.at[source, y]
+        block = gbuf.at[source, 0]
         arrived = remote(block, block, g_send.at[0, 0], g_recv.at[source], mate)
         if rz == 0:
 
@@ -160,48 +174,83 @@
             copy.start()
             sent.append(copy)
 
+    def c_round(d, dk):
+        for way in range(2):
+            c_wait(way, d - 1, dk)
+            if d < 4 or way == dk:
+                copy = c_copy(way, d, dk)
+                copy.start()
+                sent.append(copy)
+
+    def y_round(d, rz):
+        for way in range(2):
+            y_wait(way, d - 1, rz)
+            if d < 4 or way == rz // 2:
+                copy = y_copy(way, d, rz)
+                copy.start()
+                sent.append(copy)
+
     for d in range(2, 5):
         for dk in range(2):
-            for way in range(2):
-                c_wait(way, d - 1, dk)
-                if d < 4 or way == dk:
-                    copy = c_copy(way, d, dk)
-                    copy.start()
-                    sent.append(copy)
-        for rz in range(4):
-            for way in range(2):
-                y_wait(way, d - 1, rz)
-                if d < 4 or way == rz // 2:
-                    copy = y_copy(way, d, rz)
-                    copy.start()
-                    sent.append(copy)
+            c_round(d, dk)
+            for rz in (2 * dk, 2 * dk + 1):
+                y_round(d, rz)
     for way in range(2):
         c_wait(way, 4, way)
     mate_block = cbuf.at[zl, zh * 2 + 1 - c]
     remote(mate_block, mate_block, mate_send.at[0], mate_recv.at[0], mate).wait_recv()
+
+    lanes = [pl.ds(lo * 64, (hi - lo) * 64) for lo, hi in CHUNKS]
+
+    def first_part(lo, hi):
+        total = None
+        for s in range(4):
+            a = split(cbuf[s].reshape(384, 256))
+            b = split(gbuf[s, lo:hi].reshape((hi - lo) * 64, 256))
+            one = product(a, b, ((1,), (1,)))
+            total = one if total is None else total + one
+        part[:, :, lo * 64 : hi * 64] = total.reshape(4, 96, (hi - lo) * 64)
+
+    def rs_copy(i, d):
+        return remote(
+            part.at[(x + d) % 4, :, lanes[i]], parts_in.at[d - 1, :, lanes[i]],
+            rs_send.at[i, d - 1], rs_recv.at[i, d - 1], device((x + d) % 4, y, z, c),
+        )
+
+    def ag_copy(i, d, owner):
+        block = firsts.at[owner, :, lanes[i]]
+        return remote(block, block, ag_send.at[i, d - 1], ag_recv.at[i, d - 1], device((x + d) % 4, y, z, c))
+
+    def rs_start(i):
+        for d in (2, 1, 3):
+            copy = rs_copy(i, d)
+            copy.start()
+            sent.append(copy)
+
+    def rs_end(i):
+        for d in (1, 3, 2):
+            rs_copy(i, d).wait_recv()
+        span = lanes[i]
+        firsts[x, :, span] = (part[x, :, span] + parts_in[0, :, span]) + (parts_in[1, :, span] + parts_in[2, :, span])
+        for d in (2, 1, 3):
+            copy = ag_copy(i, d, x)
+            copy.start()
+            sent.append(copy)
+
+    def ag_end(i):
+        for d in (1, 3, 2):
+            ag_copy(i, d, (x + 4 - d) % 4).wait_recv()
+
+    first_part(0, 4)
+    rs_start(0)
+    first_part(4, 6)
+    rs_start(1)
     for rz in range(4):
         y_wait(rz // 2, 4, rz)
-
-    total = None
-    for s in range(4):
-        a = split(cbuf[s].reshape(384, 256))
-        b = split(gbuf[s].reshape(512, 256))
-        one = product(a, b, ((1,), (1,)))
-        total = one if total is None else total + one
-    part[...] = total.reshape(4, 96, 512)
-
-    for d in range(1, 4):
-        to = (x + d) % 4
-        copy = remote(part.at[to], parts_in.at[d - 1], rs_send.at[d - 1], rs_recv.at[d - 1], device(to, y, z, c))
-        copy.start()
-        sent.append(copy)
-    for d in range(1, 4):
-        remote(part.at[0], parts_in.at[d - 1], rs_send.at[d - 1], rs_recv.at[d - 1], mate).wait_recv()
-    firsts[x] = (part[x] + parts_in[0]) + (parts_in[1] + parts_in[2])
-    for d in range(1, 4):
-        copy = remote(firsts.at[x], firsts.at[x], ag_send.at[d - 1], ag_recv.at[d - 1], device((x + d) % 4, y, z, c))
-        copy.start()
-        sent.append(copy)
+    first_part(6, 8)
+    rs_start(2)
+    for i in range(3):
+        rs_end(i)
 
     lane = lax.broadcasted_iota(jnp.int32, (48, 128), 1)
     for t in range(4):
@@ -219,21 +268,32 @@
         def _():
             remote(fold.at[yy], fold_in.at[c, zl], fo_send.at[yy], fo_recv.at[c, zl], device(*taker(yy))).start()
 
-    for d in range(1, 4):
-        block = firsts.at[(x + 4 - d) % 4]
-        remote(block, block, ag_send.at[d - 1], ag_recv.at[d - 1], mate).wait_recv()
+    for i in range(2):
+        ag_end(i)
+        lo, hi = CHUNKS[i]
+        a = split(firsts[:, :, lanes[i]].reshape(384, (hi - lo) * 64))
+        for s in range(4):
+            b = split(gbuf[s, lo:hi].reshape((hi - lo) * 64, 256))
+            one = product(a, b, ((1,), (0,))).reshape(4, 96, 256)
+            sums[s] = one if i == 0 else sums[s] + one
+    ag_end(2)
+
+    def share(target, h):
+        return sums.at[target % 4, (target // 4) * 2 + h]
 
     def second_part(target):
-        a = split(firsts[pl.ds((target // 4) * 2, 2)].reshape(192, 512))
-        b = split(gbuf[target % 4].reshape(512, 256))
-        sums[target] = product(a, b, ((1,), (0,))).reshape(2, 96, 256)
+        lo, hi = CHUNKS[2]
+        pair = pl.ds((target // 4) * 2, 2)
+        a = split(firsts[pair, :, lanes[2]].reshape(192, (hi - lo) * 64))
+        b = split(gbuf[target % 4, lo:hi].reshape((hi - lo) * 64, 256))
+        sums[target % 4, pair] = sums[target % 4, pair] + product(a, b, ((1,), (0,))).reshape(2, 96, 256)
 
     def target_of(way, d):
         return (z + (d if way == 0 else 8 - d)) % 8
 
     def z_copy(way, d, h):
         return remote(
-            sums.at[target_of(way, d), h], sums_in.at[way, d - 1, h],
+            share(target_of(way, d), h), sums_in.at[way, d - 1, h],
             z_send.at[way, d - 1, h], z_recv.at[way, d - 1, h], device(x, y, z_step(way), c),
         )
 
@@ -244,8 +304,8 @@
 
     def z_add(way, d, h):
         z_copy(way, d, h).wait_recv()
-        target = target_of(way, d - 1)
-        sums[target, h] = sums[target, h] + sums_in[way, d - 1, h]
+        mine = share(target_of(way, d - 1), h)
+        mine[...] = mine[...] + sums_in[way, d - 1, h]
 
     second_part(target_of(0, 4))
     z_start(0, 4, 0)
@@ -270,7 +330,7 @@
         for way in range(2):
             z_add(way, 1, 1 - way if half == 0 else way)
 
-    copy = remote(sums.at[z, 1 - c], swap_in.at[0], sw_send.at[0], sw_recv.at[0], mate)
+    copy = remote(share(z, 1 - c), swap_in.at[0], sw_send.at[0], sw_recv.at[0], mate)
     copy.start()
     sent.append(copy)
 
@@ -289,7 +349,7 @@
 
     scale_mine = jnp.where(c == 0, scale[0], scale[1])
     scale_other = jnp.where(c == 0, scale[1], scale[0])
-    second_out[c] = sums[z, c] * scale_mine
+    second_out[c] = share(z, c)[...] * scale_mine
     copy.wait_recv()
     second_out[1 - c] = swap_in[0] * scale_other
 
@@ -301,7 +361,7 @@
 
             @pl.when(jnp.logical_not(is_me((x, y, zh * 4 + 2 * c + e, k))))
             def _():
-                remote(turned.at[k, pl.ds(e * 64, 64)], gbuf.at[zl, y], g_send.at[e, k], g_recv.at[0], mate).wait_send()
+                remote(turned.at[k, pl.ds(e * 64, 64)], gbuf.at[zl, 0], g_send.at[e, k], g_recv.at[0], mate).wait_send()
 
     for yy in range(8):
 
@@ -317,9 +377,15 @@
     return pl.pallas_call(
         kernel,
         out_shape=(shape, shape),
-        in_specs=[vmem] * 5,
+        in_specs=[pl.BlockSpec(memory_space=pl.ANY)] * 5,
         out_specs=(vmem, vmem),
         scratch_shapes=[
+            pltpu.VMEM((2, 96, 256), F32),
+            pltpu.VMEM((2, 256, 128), F32),
+            pltpu.VMEM((1, 1), jnp.int32),
+            pltpu.VMEM((1, 96), jnp.int32),
+            pltpu.VMEM((1, 96), jnp.int32),
+            dma((5,)),
             pltpu.VMEM((2, 96, 256), F32),
             pltpu.VMEM((2, 128, 256), F32),
             pltpu.VMEM((4, 4, 96, 256), F32),
@@ -329,21 +395,21 @@
             pltpu.VMEM((4, 96, 512), F32),
             pltpu.VMEM((8, 48, 128), F32),
             pltpu.VMEM((2, 4, 48, 128), F32),
-            pltpu.VMEM((8, 2, 96, 256), F32),
+            pltpu.VMEM((4, 4, 96, 256), F32),
             pltpu.VMEM((2, 4, 2, 96, 256), F32),
             pltpu.VMEM((1, 96, 256), F32),
             dma((2, 2)), dma((4,)),
             dma((2, 4, 2)), dma((2, 4, 2)),
             dma((1,)), dma((1,)),
             dma((2, 4, 4)), dma((2, 4, 4)),
-            dma((3,)), dma((3,)),
-            dma((3,)), dma((3,)),
+            dma((3, 3)), dma((3, 3)),
+            dma((3, 3)), dma((3, 3)),
             dma((8,)), dma((2, 4)),
             dma((2, 4, 2)), dma((2, 4, 2)),
             dma((1,)), dma((1,)),
         ],
         compiler_params=pltpu.CompilerParams(
-            collective_id=0, has_side_effects=True, vmem_limit_bytes=40 << 20
+            collective_id=0, has_side_effects=True, vmem_limit_bytes=60 << 20
         ),
         name="sigma",
     )(

time: 95.6 us -> 92.5 us (0.968)
  Pallas kernels: 90.3 us -> 88.7 us
  local copies, waits for them, and re-layouts: 3.89 us -> 2.34 us
    pallas_call x1, Pallas kernels: 90.3 us -> 88.7 us  [on_device(): pl.pallas_call(kernel, out_shape=(shape, shape), in_specs=[pl.BlockSpec(m...]
    unnamed x10 -> x4, local copies, waits for them, and re-layouts: 3.89 us -> 2.34 us
where the time goes in v2:
time: 92.5 us; the launch traced here: 92.3 us
  Pallas kernels  88.7 us (96%)
  local copies, waits for them, and re-layouts  2.34 us (3%)
  between operations  1.29 us (1%)
    pallas_call x1, Pallas kernels, on_device(): pl.pallas_call(kernel, out_shape=(shape, shape), in_specs=[pl.BlockSpec(m...  88.7 us
    unnamed x4, local copies, waits for them, and re-layouts  2.34 us

profile of v2, /device:TPU:1, one launch (start us, length us, event | category | flops | bytes accessed | tf_op | source)
XLA Modules:
  0.0 92.3 jit_solution(8686525568956683896)
XLA Ops:
  1.3 88.7 %sigma.1 = (f32[2,96,256]{2,1,0:T(8,128)}, f32[2,96,256]{2,1,0:T(8,128)}) custom-call(f32[2,96,256]{2,1,0:T(8,128)} %ci_hbm.1, f32[2,256,128]{2,1,0:T(8,128)} %integrals_hbm.1, s32[1,1]{1,0:T(1,128)} %bitcast.3.live_hbm, s32[1,96]{1,0:T(1,128)} %bitcast.4, s32[1,96]{1,0:T(1,128)} %bitcast.5), custom_call_target="tpu_custom_call" | custom-call | tf_op jit(solution)/shard_map/sigma/pallas_call | solution.py:377
  90.0 0.0 copy-start
  90.0 1.7 %copy.10 = f32[2,96,256]{2,1,0:T(8,128)} copy(f32[2,96,256]{2,1,0:T(8,128)} %get-tuple-element.4) | data formatting | bytes 393216
  91.6 0.0 copy-done
  91.6 0.7 copy.11
Async XLA Ops:
  90.0 1.7 %copy-start = (f32[2,96,256]{2,1,0:T(8,128)S(1)}, f32[2,96,256]{2,1,0:T(8,128)}, u32[]{:S(2)}) copy-start(f32[2,96,256]{2,1,0:T(8,128)} %get-tuple-element.5) | copy-start | bytes 589828

commit v3 on v2

v3 whole, which is shorter than its diff:
```python
import functools

import jax
import jax.numpy as jnp
from jax import lax
from jax.experimental import pallas as pl
from jax.experimental.pallas import tpu as pltpu
from jax.sharding import PartitionSpec as P

MESH = pl.DeviceIdType.MESH
F32 = jnp.float32
BF16 = jnp.bfloat16


def device(x, y, z, c):
    return ((z // 4) * 16 + y * 2 + c, x * 4 + z % 4)


def split(a):
    high = a.astype(BF16)
    return high, (a - high.astype(F32)).astype(BF16)


def product(a, b, dims):
    dot = functools.partial(lax.dot_general, dimension_numbers=(dims, ((), ())), preferred_element_type=F32)
    return dot(a[0], b[0]) + (dot(a[0], b[1]) + dot(a[1], b[0]))


OFFSETS = (0, -1, 1, -2, 2, -3, 3, 4)
UNITS = ((0, 0, 6), (0, 6, 8), (1, 0, 4), (1, 4, 8))


def kernel(
    ci_hbm, integrals_hbm, live_hbm, kind_hbm, sign_hbm, first_out, second_out,
    ci, integrals, live, kind, sign, in_sem, scaled, turned, cbuf, gbuf, part, parts_in, firsts, fold, fold_in, sums, sums_in, swap_in,
    g_send, g_recv, c_send, c_recv, mate_send, mate_recv, y_send, y_recv,
    rs_send, rs_recv, ag_send, ag_recv, fo_send, fo_recv, z_send, z_recv, sw_send, sw_recv,
):
    loads = [
        pltpu.make_async_copy(src, dst, in_sem.at[i])
        for i, (src, dst) in enumerate(
            zip((integrals_hbm, ci_hbm, live_hbm, kind_hbm, sign_hbm), (integrals, ci, live, kind, sign))
        )
    ]
    for load in loads:
        load.start()
    walk, slab = lax.axis_index("walk"), lax.axis_index("slab")
    x, zl = slab // 4, slab % 4
    zh, y, c = walk // 16, (walk // 2) % 8, walk % 2
    z = zh * 4 + zl

    def remote(src, dst, send, recv, to):
        return pltpu.make_async_remote_copy(
            src_ref=src, dst_ref=dst, send_sem=send, recv_sem=recv, device_id=to, device_id_type=MESH
        )

    givers = [(sub, quarter, k) for sub in range(2) for quarter in range(4) for k in range(2)]

    def giver(sub, quarter, k):
        return (2 * zh + sub, y, (x // 2) * 4 + quarter, k)

    def is_me(place):
        return (place[0] == x) & (place[1] == y) & (place[2] == z) & (place[3] == c)

    barrier = pltpu.get_barrier_semaphore()
    near = [(x, y, (z + dz) % 8, (c + dc) % 2) for dz in range(8) for dc in range(2) if dz or dc]
    near += [(x, (y + 1) % 8, z, c), (x, (y + 7) % 8, z, c)]
    near += [((x + d) % 4, y, z, c) for d in (1, 2, 3)]
    for place in near:
        pl.semaphore_signal(barrier, inc=1, device_id=device(*place), device_id_type=MESH)
    for which in givers:
        place = giver(*which)

        @pl.when(jnp.logical_not(is_me(place)))
        def _():
            pl.semaphore_signal(barrier, inc=1, device_id=device(*place), device_id_type=MESH)

    takers = [(h, slot) for h in range(2) for slot in range(8)]

    def taker(h, slot):
        yy = (y + OFFSETS[slot] + 8) % 8
        return (2 * zh + yy // 4, y, (x // 2) * 4 + yy % 4, c if h else 1 - c)

    mine = {which: is_me(taker(*which)) for which in takers}
    own = functools.reduce(lambda a, b: a + b, [m.astype(jnp.int32) for m in mine.values()])

    rows = lax.broadcasted_iota(jnp.int32, (96, 96), 0)
    cols = lax.broadcasted_iota(jnp.int32, (96, 96), 1)

    def column(line):
        return jnp.sum(jnp.where(rows == cols, jnp.broadcast_to(line, (96, 96)), 0.0), axis=1, keepdims=True)

    for load in loads:
        load.wait()
    position = lax.broadcasted_iota(jnp.int32, (1, 96), 1)
    alive = position < live[...]
    plus = jnp.where(alive & (kind[...] != 1), 1.0, 0.0).astype(F32)
    minus = jnp.where(alive & (kind[...] != 0), 1.0, 0.0).astype(F32) * (2 * sign[...] - 1).astype(F32)
    scale = [column(plus), column(minus)]
    for k in range(2):
        scaled[k] = ci[k] * scale[k]
        turned[k] = integrals[k].T
    cbuf[zl, 1, zh] = scaled[c]

    pl.semaphore_wait(barrier, len(near) + 16 - own)

    for e in range(2):
        for k in range(2):
            quarter = 2 * c + e
            to = (x, y, zh * 4 + quarter, k)
            src = turned.at[k, pl.ds(e * 64, 64)]
            here = is_me(to)

            @pl.when(here)
            def _():
                gbuf[zl, 0] = src[...]

            @pl.when(jnp.logical_not(here))
            def _():
                remote(src, gbuf.at[zl, 0], g_send.at[e, k], g_recv.at[zl], device(*to)).start()

    mate = device(x, y, z, 1 - c)
    mate_copy = remote(scaled.at[1 - c], cbuf.at[zl, 0, zh], mate_send.at[0], mate_recv.at[0], mate)
    mate_copy.start()
    sent = []

    def start(copy):
        copy.start()
        sent.append(copy)

    def z_step(way):
        return (z + (1 if way == 0 else 7)) % 8

    def y_step(way):
        return (y + (1 if way == 0 else 7)) % 8

    def c_first(h):
        k = c if h else 1 - c
        for way in range(2):
            start(remote(scaled.at[k], cbuf.at[zl, h, zh], c_send.at[way, 0, h], c_recv.at[way, 0, h], device(x, y, z_step(way), k)))

    def c_block(way, d, h):
        source = (z + (8 - d if way == 0 else d)) % 8
        return cbuf.at[source % 4, h, source // 4]

    def y_block(way, d, rz):
        slot = min(2 * d - 1 + way, 7) if d else 0
        return gbuf.at[(zl + 4 - rz) % 4, slot]

    def c_copy(way, d, h):
        block = c_block(way, d - 1, h)
        return remote(block, block, c_send.at[way, d - 1, h], c_recv.at[way, d - 1, h], device(x, y, z_step(way), c))

    def c_wait(way, d, h):
        block = c_block(way, d, h)
        remote(block, block, c_send.at[way, d - 1, h], c_recv.at[way, d - 1, h], mate).wait_recv()

    def y_copy(way, d, rz):
        return remote(
            y_block(way, d - 1, rz), y_block(way, d, rz),
            y_send.at[way, d - 1, rz], y_recv.at[way, d - 1, rz], device(x, y_step(way), z, c),
        )

    def y_wait(way, d, rz):
        block = y_block(way, d, rz)
        remote(block, block, y_send.at[way, d - 1, rz], y_recv.at[way, d - 1, rz], mate).wait_recv()

    def c_round(d, h):
        for way in range(2):
            c_wait(way, d - 1, h)
            if d < 4 or way == h:
                start(c_copy(way, d, h))

    def y_round(d, rz):
        for way in range(2):
            y_wait(way, d - 1, rz)
            if d < 4 or way == rz // 2:
                start(y_copy(way, d, rz))

    def y_first(rz):
        source = (zl + 4 - rz) % 4
        block = gbuf.at[source, 0]
        arrived = remote(block, block, g_send.at[0, 0], g_recv.at[source], mate)
        if rz == 0:

            @pl.when(c != zl // 2)
            def _():
                arrived.wait_recv()
        else:
            arrived.wait_recv()
        for way in range(2):
            start(y_copy(way, 1, rz))

    c_first(0)
    y_first(0)
    y_round(2, 0)
    for rz in (1, 2, 3):
        y_first(rz)
    c_round(2, 0)
    c_first(1)
    y_round(3, 0)
    for rz in (1, 2, 3):
        y_round(2, rz)
    c_round(3, 0)
    c_round(2, 1)
    y_round(4, 0)
    for rz in (1, 2, 3):
        y_round(3, rz)
    c_round(4, 0)
    c_round(3, 1)
    for rz in (1, 2, 3):
        y_round(4, rz)

    lanes = [pl.ds(lo * 64, (hi - lo) * 64) for _, lo, hi in UNITS]

    def first_part(i):
        h, lo, hi = UNITS[i]
        total = None
        for s in range(4):
            a = split(cbuf[s, h].reshape(192, 256))
            b = split(gbuf[s, lo:hi].reshape((hi - lo) * 64, 256))
            one = product(a, b, ((1,), (1,)))
            total = one if total is None else total + one
        part[h, :, :, lo * 64 : hi * 64] = total.reshape(4, 48, (hi - lo) * 64)
        for d in (2, 1, 3):
            start(rs_copy(i, d))

    def rs_copy(i, d):
        h = UNITS[i][0]
        return remote(
            part.at[h, (x + d) % 4, :, lanes[i]], parts_in.at[h, d - 1, :, lanes[i]],
            rs_send.at[i, d - 1], rs_recv.at[i, d - 1], device((x + d) % 4, y, z, c),
        )

    def ag_copy(i, d, owner):
        block = firsts.at[UNITS[i][0], owner, :, lanes[i]]
        return remote(block, block, ag_send.at[i, d - 1], ag_recv.at[i, d - 1], device((x + d) % 4, y, z, c))

    def rs_end(i):
        for d in (1, 3, 2):
            rs_copy(i, d).wait_recv()
        h, span = UNITS[i][0], lanes[i]
        firsts[h, x, :, span] = (part[h, x, :, span] + parts_in[h, 0, :, span]) + (
            parts_in[h, 1, :, span] + parts_in[h, 2, :, span]
        )
        for d in (2, 1, 3):
            start(ag_copy(i, d, x))

    def ag_end(i):
        for d in (1, 3, 2):
            ag_copy(i, d, (x + 4 - d) % 4).wait_recv()

    lane = lax.broadcasted_iota(jnp.int32, (24, 128), 1)

    def first_away(h):
        for t in range(4):
            tile = firsts[h, x, :, pl.ds(t * 128, 128)]
            top, low = tile[:24], tile[24:]
            fold[h, 2 * t] = jnp.where(lane < 64, top, pltpu.roll(low, 64, 1))
            fold[h, 2 * t + 1] = jnp.where(lane < 64, pltpu.roll(top, 64, 1), low)
        for slot in range(8):

            @pl.when(mine[h, slot])
            def _():
                fold_in[c, zl, x % 2] = fold[h, slot]

            @pl.when(jnp.logical_not(mine[h, slot]))
            def _():
                remote(
                    fold.at[h, slot], fold_in.at[c, zl, x % 2],
                    fo_send.at[h, slot], fo_recv.at[c, zl, x % 2], device(*taker(h, slot)),
                ).start()

    def target_of(way, d):
        return (z + (d if way == 0 else 8 - d)) % 8

    def second_early(i):
        h, lo, hi = UNITS[i]
        a = split(firsts[h, :, :, lanes[i]].reshape(192, (hi - lo) * 64))
        for s in range(4):
            b = split(gbuf[s, lo:hi].reshape((hi - lo) * 64, 256))
            sums[s, h] = product(a, b, ((1,), (0,))).reshape(2, 96, 256)

    def second_late(i, target):
        h, lo, hi = UNITS[i]
        a = split(firsts[h, pl.ds((target // 4) * 2, 2), :, lanes[i]].reshape(96, (hi - lo) * 64))
        b = split(gbuf[target % 4, lo:hi].reshape((hi - lo) * 64, 256))
        sums[target % 4, h, target // 4] = sums[target % 4, h, target // 4] + product(a, b, ((1,), (0,)))

    def z_copy(h, way, d, j):
        target = target_of(way, d)
        return remote(
            sums.at[target % 4, h, target // 4, pl.ds(j * 48, 48)], sums_in.at[h, way, d - 1, pl.ds(j * 48, 48)],
            z_send.at[h, way, d - 1, j], z_recv.at[h, way, d - 1, j], device(x, y, z_step(way), c),
        )

    def z_add(h, way, d, j):
        z_copy(h, way, d, j).wait_recv()
        target, rows = target_of(way, d - 1), pl.ds(j * 48, 48)
        sums[target % 4, h, target // 4, rows] = (
            sums[target % 4, h, target // 4, rows] + sums_in[h, way, d - 1, rows]
        )

    def z_begin(i):
        h = UNITS[i][0]
        long, short = (0, 1) if h == 0 else (1, 0)
        for way, d in ((long, 4), (short, 3)):
            second_late(i, target_of(way, d))
            for j in range(2):
                start(z_copy(h, way, d, j))
        for d in (3, 2, 1):
            second_late(i, target_of(long, d))
            if d < 3:
                second_late(i, target_of(short, d))
        second_late(i, z)

    def z_round(h, r):
        long, short = (0, 1) if h == 0 else (1, 0)
        for j in range(2):
            for way, d in ((long, 5 - r), (short, 4 - r)):
                if d >= 1:
                    z_add(h, way, d, j)
                    if d > 1:
                        start(z_copy(h, way, d - 1, j))

    for way in range(2):
        if way == 0:
            c_wait(way, 4, 0)
    mate_block = cbuf.at[zl, 0, zh]
    remote(mate_block, mate_block, mate_send.at[0], mate_recv.at[0], mate).wait_recv()
    first_part(0)
    c_round(4, 1)
    for rz in range(4):
        y_wait(rz // 2, 4, rz)
    first_part(1)
    c_wait(1, 4, 1)
    first_part(2)
    rs_end(0)
    rs_end(1)
    first_part(3)
    first_away(0)
    ag_end(0)
    second_early(0)
    rs_end(2)
    ag_end(1)
    z_begin(1)
    rs_end(3)
    first_away(1)
    z_round(0, 1)
    ag_end(2)
    second_early(2)
    z_round(0, 2)
    ag_end(3)
    z_begin(3)
    z_round(0, 3)
    z_round(1, 1)
    z_round(0, 4)
    swap = remote(sums.at[zl, 0, zh], swap_in.at[0], sw_send.at[0], sw_recv.at[0], mate)
    start(swap)
    z_round(1, 2)

    for which in givers:
        sub, quarter, k = which
        block = fold_in.at[k, quarter, sub]

        @pl.when(jnp.logical_not(is_me(giver(*which))))
        def _():
            remote(block, block, fo_send.at[0, 0], fo_recv.at[k, quarter, sub], mate).wait_recv()

    for k in range(2):
        for sub in range(2):
            for t in range(2):
                left, right = fold_in[k, 2 * t, sub], fold_in[k, 2 * t + 1, sub]
                rows, span = sub * 48, slice(t * 128, t * 128 + 128)
                first_out[k, rows : rows + 24, span] = jnp.where(lane < 64, left, pltpu.roll(right, 64, 1))
                first_out[k, rows + 24 : rows + 48, span] = jnp.where(lane < 64, pltpu.roll(left, 64, 1), right)

    z_round(1, 3)
    z_round(1, 4)
    scale_mine = jnp.where(c == 0, scale[0], scale[1])
    scale_other = jnp.where(c == 0, scale[1], scale[0])
    second_out[c] = sums[zl, 1, zh] * scale_mine
    swap.wait_recv()
    second_out[1 - c] = swap_in[0] * scale_other

    for copy in sent:
        copy.wait_send()
    mate_copy.wait_send()
    for e in range(2):
        for k in range(2):

            @pl.when(jnp.logical_not(is_me((x, y, zh * 4 + 2 * c + e, k))))
            def _():
                remote(turned.at[k, pl.ds(e * 64, 64)], gbuf.at[zl, 0], g_send.at[e, k], g_recv.at[0], mate).wait_send()

    for which in takers:

        @pl.when(jnp.logical_not(mine[which]))
        def _():
            remote(fold.at[which], fold_in.at[0, 0, 0], fo_send.at[which], fo_recv.at[0, 0, 0], mate).wait_send()


def on_device(ci_blocks, integrals, live_counts, walk_kind, walk_sign):
    vmem = pl.BlockSpec(memory_space=pltpu.VMEM)
    dma = pltpu.SemaphoreType.DMA
    shape = jax.ShapeDtypeStruct((2, 96, 256), F32)
    return pl.pallas_call(
        kernel,
        out_shape=(shape, shape),
        in_specs=[pl.BlockSpec(memory_space=pl.ANY)] * 5,
        out_specs=(vmem, vmem),
        scratch_shapes=[
            pltpu.VMEM((2, 96, 256), F32),
            pltpu.VMEM((2, 256, 128), F32),
            pltpu.VMEM((1, 1), jnp.int32),
            pltpu.VMEM((1, 96), jnp.int32),
            pltpu.VMEM((1, 96), jnp.int32),
            dma((5,)),
            pltpu.VMEM((2, 96, 256), F32),
            pltpu.VMEM((2, 128, 256), F32),
            pltpu.VMEM((4, 2, 2, 96, 256), F32),
            pltpu.VMEM((4, 8, 64, 256), F32),
            pltpu.VMEM((2, 4, 48, 512), F32),
            pltpu.VMEM((2, 3, 48, 512), F32),
            pltpu.VMEM((2, 4, 48, 512), F32),
            pltpu.VMEM((2, 8, 24, 128), F32),
            pltpu.VMEM((2, 4, 2, 24, 128), F32),
            pltpu.VMEM((4, 2, 2, 96, 256), F32),
            pltpu.VMEM((2, 2, 4, 96, 256), F32),
            pltpu.VMEM((1, 96, 256), F32),
            dma((2, 2)), dma((4,)),
            dma((2, 4, 2)), dma((2, 4, 2)),
            dma((1,)), dma((1,)),
            dma((2, 4, 4)), dma((2, 4, 4)),
            dma((4, 3)), dma((4, 3)),
            dma((4, 3)), dma((4, 3)),
            dma((2, 8)), dma((2, 4, 2)),
            dma((2, 2, 4, 2)), dma((2, 2, 4, 2)),
            dma((1,)), dma((1,)),
        ],
        compiler_params=pltpu.CompilerParams(
            collective_id=0, has_side_effects=True, vmem_limit_bytes=60 << 20
        ),
        name="sigma",
    )(
        ci_blocks, integrals, live_counts.reshape(1, 1),
        walk_kind.reshape(1, 96), walk_sign.reshape(1, 96),
    )


def solution(mesh):
    placed = (P(None, "walk", "slab"), P(None, "slab", "walk"), P("walk"), P("walk"), P("walk"))
    return jax.shard_map(
        on_device,
        mesh=mesh,
        in_specs=placed,
        out_specs=(P(None, "walk", "slab"), P(None, "walk", "slab")),
        check_vma=False,
    )
```

time: 92.5 us -> 89.1 us (0.963)
  the two profiles are of different devices: /device:TPU:1 before, /device:TPU:6 now
where the time goes in v3:
time: 89.1 us; the launch traced here: 89 us
  Pallas kernels  85.3 us (96%)
  local copies, waits for them, and re-layouts  2.34 us (3%)
  between operations  1.29 us (1%)
    pallas_call x1, Pallas kernels, on_device(): pl.pallas_call(kernel, out_shape=(shape, shape), in_specs=[pl.BlockSpec(m...  85.3 us
    unnamed x4, local copies, waits for them, and re-layouts  2.34 us

profile of v3, /device:TPU:6, one launch (start us, length us, event | category | flops | bytes accessed | tf_op | source)
XLA Modules:
  0.0 89.0 jit_solution(13201527410482246952)
XLA Ops:
  1.3 85.3 %sigma.1 = (f32[2,96,256]{2,1,0:T(8,128)}, f32[2,96,256]{2,1,0:T(8,128)}) custom-call(f32[2,96,256]{2,1,0:T(8,128)} %ci_hbm.1, f32[2,256,128]{2,1,0:T(8,128)} %integrals_hbm.1, s32[1,1]{1,0:T(1,128)} %bitcast.3.live_hbm, s32[1,96]{1,0:T(1,128)} %bitcast.4, s32[1,96]{1,0:T(1,128)} %bitcast.5), custom_call_target="tpu_custom_call" | custom-call | tf_op jit(solution)/shard_map/sigma/pallas_call | solution.py:407
  86.6 0.0 copy-start
  86.6 1.7 %copy.10 = f32[2,96,256]{2,1,0:T(8,128)} copy(f32[2,96,256]{2,1,0:T(8,128)} %get-tuple-element.4) | data formatting | bytes 393216
  88.3 0.0 copy-done
  88.3 0.7 copy.11
Async XLA Ops:
  86.6 1.7 %copy-start = (f32[2,96,256]{2,1,0:T(8,128)S(1)}, f32[2,96,256]{2,1,0:T(8,128)}, u32[]{:S(2)}) copy-start(f32[2,96,256]{2,1,0:T(8,128)} %get-tuple-element.5) | copy-start | bytes 589828

commit v4 on v0

v4 whole, which is shorter than its diff:
```python
import functools

import jax
import jax.numpy as jnp
from jax import lax
from jax.experimental import pallas as pl
from jax.experimental.pallas import tpu as pltpu
from jax.sharding import PartitionSpec as P

MESH = pl.DeviceIdType.MESH
F32 = jnp.float32
BF16 = jnp.bfloat16


def device(x, y, z, c):
    return ((z // 4) * 16 + y * 2 + c, x * 4 + z % 4)


def split(a):
    high = a.astype(BF16)
    return high, (a - high.astype(F32)).astype(BF16)


def product(a, b, dims):
    dot = functools.partial(lax.dot_general, dimension_numbers=(dims, ((), ())), preferred_element_type=F32)
    return dot(a[0], b[0]) + (dot(a[0], b[1]) + dot(a[1], b[0]))


OFFSETS = (0, -1, 1, -2, 2, -3, 3, 4)
UNITS = ((0, 0, 6), (0, 6, 8), (1, 0, 6), (1, 6, 8))


def kernel(
    ci_hbm, integrals_hbm, live_hbm, kind_hbm, sign_hbm, first_out, second_out,
    ci, integrals, live, kind, sign, in_sem, turned, cbuf, gbuf, part, parts_in, firsts, fold, fold_in, sums, sums_in,
    g_send, g_recv, c_send, c_recv, m_send, m_recv, y_send, y_recv,
    rs_send, rs_recv, ag_send, ag_recv, fo_send, fo_recv, z_send, z_recv,
):
    loads = [
        pltpu.make_async_copy(src, dst, in_sem.at[i])
        for i, (src, dst) in enumerate(
            zip((integrals_hbm, ci_hbm, live_hbm, kind_hbm, sign_hbm), (integrals, ci, live, kind, sign))
        )
    ]
    for load in loads:
        load.start()
    walk, slab = lax.axis_index("walk"), lax.axis_index("slab")
    x, zl = slab // 4, slab % 4
    zh, y, c = walk // 16, (walk // 2) % 8, walk % 2
    z = zh * 4 + zl

    def remote(src, dst, send, recv, to):
        return pltpu.make_async_remote_copy(
            src_ref=src, dst_ref=dst, send_sem=send, recv_sem=recv, device_id=to, device_id_type=MESH
        )

    givers = [(sub, quarter) for sub in range(2) for quarter in range(4)]

    def giver(sub, quarter):
        return (2 * zh + sub, y, (x // 2) * 4 + quarter, c)

    def is_me(place):
        return (place[0] == x) & (place[1] == y) & (place[2] == z) & (place[3] == c)

    barrier = pltpu.get_barrier_semaphore()
    near = [(x, y, (z + dz) % 8, (c + dc) % 2) for dz in range(8) for dc in range(2) if dz or dc]
    near += [(x, (y + 1) % 8, z, c), (x, (y + 7) % 8, z, c)]
    near += [((x + d) % 4, y, z, c) for d in (1, 2, 3)]
    for place in near:
        pl.semaphore_signal(barrier, inc=1, device_id=device(*place), device_id_type=MESH)
    for which in givers:
        place = giver(*which)

        @pl.when(jnp.logical_not(is_me(place)))
        def _():
            pl.semaphore_signal(barrier, inc=1, device_id=device(*place), device_id_type=MESH)

    def taker(slot):
        yy = (y + OFFSETS[slot] + 8) % 8
        return (2 * zh + yy // 4, y, (x // 2) * 4 + yy % 4, c)

    mine = [is_me(taker(slot)) for slot in range(8)]
    own = functools.reduce(lambda a, b: a + b, [m.astype(jnp.int32) for m in mine])

    rows = lax.broadcasted_iota(jnp.int32, (96, 96), 0)
    cols = lax.broadcasted_iota(jnp.int32, (96, 96), 1)

    def column(line):
        return jnp.sum(jnp.where(rows == cols, jnp.broadcast_to(line, (96, 96)), 0.0), axis=1, keepdims=True)

    for load in loads:
        load.wait()
    position = lax.broadcasted_iota(jnp.int32, (1, 96), 1)
    alive = position < live[...]
    plus = jnp.where(alive & (kind[...] != 1), 1.0, 0.0).astype(F32)
    minus = jnp.where(alive & (kind[...] != 0), 1.0, 0.0).astype(F32) * (2 * sign[...] - 1).astype(F32)
    scale = [column(plus), column(minus)]
    for k in range(2):
        cbuf[k, zl, zh] = ci[k] * scale[k]
        turned[k] = integrals[k].T

    pl.semaphore_wait(barrier, len(near) + 8 - own)

    mate = device(x, y, z, 1 - c)
    sent = []

    def start(copy):
        copy.start()
        sent.append(copy)

    def z_step(way):
        return (z + (1 if way == 0 else 7)) % 8

    def y_step(way):
        return (y + (1 if way == 0 else 7)) % 8

    pieces = [(e, half) for e in range(2) for half in range(2)]

    def quarter_of(e, half):
        return (x, y, zh * 4 + 2 * c + e, half)

    def g_copy(k, e, half):
        return remote(
            turned.at[k, pl.ds(e * 64 + half * 32, 32)], gbuf.at[k, 0, half, (2 * c + e + 4 - zl) % 4],
            g_send.at[k, e, half], g_recv.at[k, (2 * c + e + 4 - zl) % 4], device(*quarter_of(e, half)),
        )

    def g_first(k):
        for e, half in pieces:
            here = is_me(quarter_of(e, half))

            @pl.when(here)
            def _():
                gbuf[k, 0, half, 0] = turned[k, e * 64 + half * 32 : e * 64 + half * 32 + 32]

            @pl.when(jnp.logical_not(here))
            def _():
                g_copy(k, e, half).start()

    def g_wait(k, rz):
        block = gbuf.at[k, 0, c, rz]
        arrived = remote(block, block, g_send.at[k, 0, 0], g_recv.at[k, rz], mate)
        if rz == 0:

            @pl.when(c != zl // 2)
            def _():
                arrived.wait_recv()
        else:
            arrived.wait_recv()

    def c_block(k, way, d, j):
        source = (z + (8 - d if way == 0 else d)) % 8
        return cbuf.at[k, source % 4, source // 4, pl.ds(j * 48, 48)]

    def c_start(k, d):
        for j in range(2):
            for way in range(2):
                if d < 4 or way == j:
                    block = c_block(k, way, d - 1, j)
                    if d > 1:
                        c_wait(k, way, d - 1, j)
                    start(remote(
                        block, block, c_send.at[k, way, d - 1, j], c_recv.at[k, way, d - 1, j],
                        device(x, y, z_step(way), c),
                    ))
                else:
                    c_wait(k, way, d - 1, j)

    def c_wait(k, way, d, j):
        block = c_block(k, way, d, j)
        remote(block, block, c_send.at[k, way, d - 1, j], c_recv.at[k, way, d - 1, j], mate).wait_recv()

    def y_block(k, way, d, rz):
        slot = min(2 * d - 1 + way, 7) if d else 0
        return gbuf.at[k, slot, c, rz]

    def y_wait(k, way, d, rz):
        block = y_block(k, way, d, rz)
        remote(block, block, y_send.at[k, way, d - 1, rz], y_recv.at[k, way, d - 1, rz], mate).wait_recv()

    def y_start(k, d, *chunks):
        for rz in chunks:
            if d == 1:
                g_wait(k, rz)
            for way in range(2):
                if d > 1:
                    y_wait(k, way, d - 1, rz)
                if d < 4 or way == rz // 2:
                    start(remote(
                        y_block(k, way, d - 1, rz), y_block(k, way, d, rz),
                        y_send.at[k, way, d - 1, rz], y_recv.at[k, way, d - 1, rz], device(x, y_step(way), z, c),
                    ))
        if chunks[-1] == 3:
            for slot in (0,) if d == 1 else (2 * d - 3, 2 * d - 2):
                m_start(k, slot)

    def y_end(k):
        for rz in range(4):
            y_wait(k, rz // 2, 4, rz)
        m_start(k, 7)

    def m_start(k, slot):
        block = gbuf.at[k, slot, c]
        start(remote(block, block, m_send.at[k, slot], m_recv.at[k, slot], mate))

    def m_end(k, lo, hi):
        for slot in range(lo, hi):
            block = gbuf.at[k, slot, 1 - c]
            remote(block, block, m_send.at[k, slot], m_recv.at[k, slot], mate).wait_recv()

    lanes = [pl.ds(lo * 64, (hi - lo) * 64) for _, lo, hi in UNITS]

    def g_tile(k, lo, hi, rz):
        return split(gbuf[k, lo:hi, :, rz].reshape((hi - lo) * 64, 256))

    def first_part(i):
        k, lo, hi = UNITS[i]
        m_end(k, lo, hi)
        total = None
        for rz in range(4):
            a = split(cbuf[k, (zl + 4 - rz) % 4].reshape(192, 256))
            one = product(a, g_tile(k, lo, hi, rz), ((1,), (1,)))
            total = one if total is None else total + one
        part[k, :, :, lo * 64 : hi * 64] = total.reshape(4, 48, (hi - lo) * 64)
        for d in (2, 1, 3):
            start(rs_copy(i, d))

    def rs_copy(i, d):
        h = UNITS[i][0]
        return remote(
            part.at[h, (x + d) % 4, :, lanes[i]], parts_in.at[h, d - 1, :, lanes[i]],
            rs_send.at[i, d - 1], rs_recv.at[i, d - 1], device((x + d) % 4, y, z, c),
        )

    def ag_copy(i, d, owner):
        block = firsts.at[UNITS[i][0], owner, :, lanes[i]]
        return remote(block, block, ag_send.at[i, d - 1], ag_recv.at[i, d - 1], device((x + d) % 4, y, z, c))

    def rs_end(i):
        for d in (1, 3, 2):
            rs_copy(i, d).wait_recv()
        h, span = UNITS[i][0], lanes[i]
        firsts[h, x, :, span] = (part[h, x, :, span] + parts_in[h, 0, :, span]) + (
            parts_in[h, 1, :, span] + parts_in[h, 2, :, span]
        )
        for d in (2, 1, 3):
            start(ag_copy(i, d, x))

    def ag_end(i):
        for d in (1, 3, 2):
            ag_copy(i, d, (x + 4 - d) % 4).wait_recv()

    lane = lax.broadcasted_iota(jnp.int32, (24, 128), 1)

    def first_away(k):
        for t in range(4):
            tile = firsts[k, x, :, pl.ds(t * 128, 128)]
            top, low = tile[:24], tile[24:]
            fold[k, 2 * t] = jnp.where(lane < 64, top, pltpu.roll(low, 64, 1))
            fold[k, 2 * t + 1] = jnp.where(lane < 64, pltpu.roll(top, 64, 1), low)
        for slot in range(8):

            @pl.when(mine[slot])
            def _():
                fold_in[k, zl, x % 2] = fold[k, slot]

            @pl.when(jnp.logical_not(mine[slot]))
            def _():
                remote(
                    fold.at[k, slot], fold_in.at[k, zl, x % 2],
                    fo_send.at[k, slot], fo_recv.at[k, zl, x % 2], device(*taker(slot)),
                ).start()

    def target_of(way, d):
        return (z + (d if way == 0 else 8 - d)) % 8

    def second_early(i):
        k, lo, hi = UNITS[i]
        a = split(firsts[k, :, :, lanes[i]].reshape(192, (hi - lo) * 64))
        for rz in range(4):
            one = product(a, g_tile(k, lo, hi, rz), ((1,), (0,)))
            sums[k, (zl + 4 - rz) % 4] = one.reshape(2, 96, 256)

    def second_late(i, target):
        k, lo, hi = UNITS[i]
        a = split(firsts[k, pl.ds((target // 4) * 2, 2), :, lanes[i]].reshape(96, (hi - lo) * 64))
        b = g_tile(k, lo, hi, (zl + 4 - target % 4) % 4)
        sums[k, target % 4, target // 4] = sums[k, target % 4, target // 4] + product(a, b, ((1,), (0,)))

    def z_copy(k, way, d, j):
        target, rows = target_of(way, d), pl.ds(j * 48, 48)
        return remote(
            sums.at[k, target % 4, target // 4, rows], sums_in.at[k, way, d - 1, rows],
            z_send.at[k, way, d - 1, j], z_recv.at[k, way, d - 1, j], device(x, y, z_step(way), c),
        )

    def z_add(k, way, d, j):
        z_copy(k, way, d, j).wait_recv()
        target, rows = target_of(way, d - 1), pl.ds(j * 48, 48)
        sums[k, target % 4, target // 4, rows] = (
            sums[k, target % 4, target // 4, rows] + sums_in[k, way, d - 1, rows]
        )

    def z_begin(i):
        k = UNITS[i][0]
        second_late(i, target_of(0, 4))
        for way in range(2):
            start(z_copy(k, way, 4, way))
        for way in range(2):
            second_late(i, target_of(way, 3))
            start(z_copy(k, way, 3, 1 - way))
        for d in (2, 1):
            for way in range(2):
                second_late(i, target_of(way, d))
        second_late(i, z)

    def z_round(k, r):
        d = 5 - r
        for turn in range(2):
            for way in range(2):
                j = 1 - way if turn == 0 else way
                if d < 4 or j == way:
                    z_add(k, way, d, j)
                    if d > 1:
                        start(z_copy(k, way, d - 1, j))

    def drain():
        while sent:
            sent.pop().wait_send()

    def first_here(k):
        for which in givers:
            sub, quarter = which
            block = fold_in.at[k, quarter, sub]

            @pl.when(jnp.logical_not(is_me(giver(*which))))
            def _():
                remote(block, block, fo_send.at[0, 0], fo_recv.at[k, quarter, sub], mate).wait_recv()

        for sub in range(2):
            for t in range(2):
                left, right = fold_in[k, 2 * t, sub], fold_in[k, 2 * t + 1, sub]
                rows, span = sub * 48, slice(t * 128, t * 128 + 128)
                first_out[k, rows : rows + 24, span] = jnp.where(lane < 64, left, pltpu.roll(right, 64, 1))
                first_out[k, rows + 24 : rows + 48, span] = jnp.where(lane < 64, pltpu.roll(left, 64, 1), right)

    g_first(0)
    c_start(0, 1)
    g_first(1)
    y_start(0, 1, 0)
    y_start(1, 1, 0)
    y_start(0, 2, 0)
    y_start(1, 2, 0)
    c_start(0, 2)
    y_start(0, 1, 1, 2, 3)
    y_start(0, 3, 0)
    y_start(1, 3, 0)
    c_start(1, 1)
    y_start(1, 1, 1, 2, 3)
    c_start(0, 3)
    y_start(0, 2, 1, 2, 3)
    y_start(0, 4, 0)
    y_start(1, 4, 0)
    y_start(0, 3, 1, 2, 3)
    c_start(0, 4)
    c_start(1, 2)
    y_start(1, 2, 1, 2, 3)
    y_start(0, 4, 1, 2, 3)
    c_start(1, 3)
    y_start(1, 3, 1, 2, 3)
    for way in range(2):
        c_wait(0, way, 4, way)
    first_part(0)
    y_end(0)
    c_start(1, 4)
    y_start(1, 4, 1, 2, 3)
    first_part(1)
    rs_end(0)
    for way in range(2):
        c_wait(1, way, 4, way)
    first_part(2)
    rs_end(1)
    y_end(1)
    first_part(3)
    ag_end(0)
    second_early(0)
    rs_end(2)
    first_away(0)
    ag_end(1)
    z_begin(1)
    rs_end(3)
    z_round(0, 1)
    first_away(1)
    ag_end(2)
    second_early(2)
    ag_end(3)
    z_begin(3)
    z_round(0, 2)
    drain()
    z_round(0, 3)
    z_round(1, 1)
    first_here(0)
    z_round(0, 4)
    second_out[0] = sums[0, zl, zh] * scale[0]
    z_round(1, 2)
    first_here(1)
    drain()
    z_round(1, 3)
    z_round(1, 4)
    second_out[1] = sums[1, zl, zh] * scale[1]
    drain()

    for k in range(2):
        for e, half in pieces:

            @pl.when(jnp.logical_not(is_me(quarter_of(e, half))))
            def _():
                g_copy(k, e, half).wait_send()

        for slot in range(8):

            @pl.when(jnp.logical_not(mine[slot]))
            def _():
                remote(fold.at[k, slot], fold_in.at[0, 0, 0], fo_send.at[k, slot], fo_recv.at[0, 0, 0], mate).wait_send()


def on_device(ci_blocks, integrals, live_counts, walk_kind, walk_sign):
    vmem = pl.BlockSpec(memory_space=pltpu.VMEM)
    dma = pltpu.SemaphoreType.DMA
    shape = jax.ShapeDtypeStruct((2, 96, 256), F32)
    return pl.pallas_call(
        kernel,
        out_shape=(shape, shape),
        in_specs=[pl.BlockSpec(memory_space=pltpu.HBM)] * 5,
        out_specs=(vmem, vmem),
        scratch_shapes=[
            pltpu.VMEM((2, 96, 256), F32),
            pltpu.VMEM((2, 256, 128), F32),
            pltpu.VMEM((1, 1), jnp.int32),
            pltpu.VMEM((1, 96), jnp.int32),
            pltpu.VMEM((1, 96), jnp.int32),
            dma((5,)),
            pltpu.VMEM((2, 128, 256), F32),
            pltpu.VMEM((2, 4, 2, 96, 256), F32),
            pltpu.VMEM((2, 8, 2, 4, 32, 256), F32),
            pltpu.VMEM((2, 4, 48, 512), F32),
            pltpu.VMEM((2, 3, 48, 512), F32),
            pltpu.VMEM((2, 4, 48, 512), F32),
            pltpu.VMEM((2, 8, 24, 128), F32),
            pltpu.VMEM((2, 4, 2, 24, 128), F32),
            pltpu.VMEM((2, 4, 2, 96, 256), F32),
            pltpu.VMEM((2, 2, 4, 96, 256), F32),
            dma((2, 2, 2)), dma((2, 4)),
            dma((2, 2, 4, 2)), dma((2, 2, 4, 2)),
            dma((2, 8)), dma((2, 8)),
            dma((2, 2, 4, 4)), dma((2, 2, 4, 4)),
            dma((4, 3)), dma((4, 3)),
            dma((4, 3)), dma((4, 3)),
            dma((2, 8)), dma((2, 4, 2)),
            dma((2, 2, 4, 2)), dma((2, 2, 4, 2)),
        ],
        compiler_params=pltpu.CompilerParams(
            collective_id=0, has_side_effects=True, vmem_limit_bytes=60 << 20
        ),
        name="sigma",
    )(
        ci_blocks, integrals, live_counts.reshape(1, 1),
        walk_kind.reshape(1, 96), walk_sign.reshape(1, 96),
    )


def solution(mesh):
    placed = (P(None, "walk", "slab"), P(None, "slab", "walk"), P("walk"), P("walk"), P("walk"))
    return jax.shard_map(
        on_device,
        mesh=mesh,
        in_specs=placed,
        out_specs=(P(None, "walk", "slab"), P(None, "walk", "slab")),
        check_vma=False,
    )
```

time: 376 us -> 87.3 us (0.23); the launches traced: 370 us -> 87.1 us
  waiting for transfers between devices: 329 us -> 0 us
  Pallas kernels: 0 us -> 83.5 us
  matrix products: 25.6 us -> 0 us
  between operations: 14.4 us -> 1.29 us
    all_gather x3 -> x0, waiting for transfers between devices: 328 us -> none  [the longest x1 148 us: on_device(): rows = lax.all_gather(integrals, 'walk', axis=2, tiled=True)]
    pallas_call x0 -> x1, Pallas kernels: none -> 83.5 us  [on_device(): pl.pallas_call(kernel, out_shape=(shape, shape), in_specs=[pl.BlockSpec(m...]
    dot_general x2 -> x0, matrix products: 25.6 us -> none  [add_columns(): jnp.einsum('kwn,kpn->kwp', piece, rows, precision=lax.Precision.HIGHEST)]
  transfers between devices with their start and end apart: 3 -> 0, of which waited for: 3 -> 0; matrix products, arithmetic and copies ran while one was open for 0% -> 0% of each run, Pallas kernels for 0% -> 0%
where the time goes in v4:
time: 87.3 us; the launch traced here: 87.1 us
  Pallas kernels  83.5 us (96%)
  local copies, waits for them, and re-layouts  2.34 us (3%)
  between operations  1.29 us (1%)
    pallas_call x1, Pallas kernels, on_device(): pl.pallas_call(kernel, out_shape=(shape, shape), in_specs=[pl.BlockSpec(m...  83.5 us
    unnamed x4, local copies, waits for them, and re-layouts  2.34 us

profile of v4, /device:TPU:6, one launch (start us, length us, event | category | flops | bytes accessed | tf_op | source)
XLA Modules:
  0.0 87.1 jit_solution(6734353778660295336)
XLA Ops:
  1.3 83.5 %sigma.1 = (f32[2,96,256]{2,1,0:T(8,128)}, f32[2,96,256]{2,1,0:T(8,128)}) custom-call(f32[2,96,256]{2,1,0:T(8,128)} %ci_hbm.1, f32[2,256,128]{2,1,0:T(8,128)} %integrals_hbm.1, s32[1,1]{1,0:T(1,128)} %bitcast.3.live_hbm, s32[1,96]{1,0:T(1,128)} %bitcast.4, s32[1,96]{1,0:T(1,128)} %bitcast.5), custom_call_target="tpu_custom_call" | custom-call | tf_op jit(solution)/shard_map/sigma/pallas_call | solution.py:431
  84.8 0.0 copy-start
  84.8 1.7 %copy.10 = f32[2,96,256]{2,1,0:T(8,128)} copy(f32[2,96,256]{2,1,0:T(8,128)} %get-tuple-element.4) | data formatting | bytes 393216
  86.4 0.0 copy-done
  86.4 0.7 copy.11
Async XLA Ops:
  84.8 1.7 %copy-start = (f32[2,96,256]{2,1,0:T(8,128)S(1)}, f32[2,96,256]{2,1,0:T(8,128)}, u32[]{:S(2)}) copy-start(f32[2,96,256]{2,1,0:T(8,128)} %get-tuple-element.5) | copy-start | bytes 589828

commit v5 on v4

--- a/solution.py
+++ b/solution.py
@@ -395,17 +395,16 @@
     second_early(2)
     ag_end(3)
     z_begin(3)
+    z_round(1, 1)
     z_round(0, 2)
+    z_round(1, 2)
+    z_round(0, 3)
+    z_round(1, 3)
+    first_here(0)
     drain()
-    z_round(0, 3)
-    z_round(1, 1)
-    first_here(0)
     z_round(0, 4)
     second_out[0] = sums[0, zl, zh] * scale[0]
-    z_round(1, 2)
     first_here(1)
-    drain()
-    z_round(1, 3)
     z_round(1, 4)
     second_out[1] = sums[1, zl, zh] * scale[1]
     drain()

time: 87.3 us -> 84.4 us (0.967)
  the two profiles are of different devices: /device:TPU:6 before, /device:TPU:2 now
where the time goes in v5:
time: 84.4 us; the launch traced here: 84.2 us
  Pallas kernels  80.6 us (95%)
  local copies, waits for them, and re-layouts  2.34 us (3%)
  between operations  1.29 us (2%)
    pallas_call x1, Pallas kernels, on_device(): pl.pallas_call(kernel, out_shape=(shape, shape), in_specs=[pl.BlockSpec(m...  80.6 us
    unnamed x4, local copies, waits for them, and re-layouts  2.34 us

profile of v5, /device:TPU:2, one launch (start us, length us, event | category | flops | bytes accessed | tf_op | source)
XLA Modules:
  0.0 84.2 jit_solution(15807148453496960412)
XLA Ops:
  1.3 80.6 %sigma.1 = (f32[2,96,256]{2,1,0:T(8,128)}, f32[2,96,256]{2,1,0:T(8,128)}) custom-call(f32[2,96,256]{2,1,0:T(8,128)} %ci_hbm.1, f32[2,256,128]{2,1,0:T(8,128)} %integrals_hbm.1, s32[1,1]{1,0:T(1,128)} %bitcast.3.live_hbm, s32[1,96]{1,0:T(1,128)} %bitcast.4, s32[1,96]{1,0:T(1,128)} %bitcast.5), custom_call_target="tpu_custom_call" | custom-call | tf_op jit(solution)/shard_map/sigma/pallas_call | solution.py:430
  81.9 0.0 copy-start
  81.9 1.7 %copy.10 = f32[2,96,256]{2,1,0:T(8,128)} copy(f32[2,96,256]{2,1,0:T(8,128)} %get-tuple-element.4) | data formatting | bytes 393216
  83.5 0.0 copy-done
  83.5 0.7 copy.11
Async XLA Ops:
  81.9 1.7 %copy-start = (f32[2,96,256]{2,1,0:T(8,128)S(1)}, f32[2,96,256]{2,1,0:T(8,128)}, u32[]{:S(2)}) copy-start(f32[2,96,256]{2,1,0:T(8,128)} %get-tuple-element.5) | copy-start | bytes 589828

commit v6 on v5

--- a/solution.py
+++ b/solution.py
@@ -382,13 +382,13 @@
     rs_end(1)
     y_end(1)
     first_part(3)
+    rs_end(2)
+    first_away(0)
     ag_end(0)
     second_early(0)
-    rs_end(2)
-    first_away(0)
+    rs_end(3)
     ag_end(1)
     z_begin(1)
-    rs_end(3)
     z_round(0, 1)
     first_away(1)
     ag_end(2)

time: 84.4 us -> 84.5 us (level)
  the two profiles are of different devices: /device:TPU:2 before, /device:TPU:6 now
where the time goes in v6:
time: 84.5 us; the launch traced here: 83.6 us
  Pallas kernels  80 us (95%)
  local copies, waits for them, and re-layouts  2.34 us (3%)
  between operations  1.29 us (2%)
    pallas_call x1, Pallas kernels, on_device(): pl.pallas_call(kernel, out_shape=(shape, shape), in_specs=[pl.BlockSpec(m...  80 us
    unnamed x4, local copies, waits for them, and re-layouts  2.34 us

profile of v6, /device:TPU:6, one launch (start us, length us, event | category | flops | bytes accessed | tf_op | source)
XLA Modules:
  0.0 83.6 jit_solution(7052026610953140799)
XLA Ops:
  1.3 80.0 %sigma.1 = (f32[2,96,256]{2,1,0:T(8,128)}, f32[2,96,256]{2,1,0:T(8,128)}) custom-call(f32[2,96,256]{2,1,0:T(8,128)} %ci_hbm.1, f32[2,256,128]{2,1,0:T(8,128)} %integrals_hbm.1, s32[1,1]{1,0:T(1,128)} %bitcast.3.live_hbm, s32[1,96]{1,0:T(1,128)} %bitcast.4, s32[1,96]{1,0:T(1,128)} %bitcast.5), custom_call_target="tpu_custom_call" | custom-call | tf_op jit(solution)/shard_map/sigma/pallas_call | solution.py:430
  81.2 0.0 copy-start
  81.3 1.7 %copy.10 = f32[2,96,256]{2,1,0:T(8,128)} copy(f32[2,96,256]{2,1,0:T(8,128)} %get-tuple-element.4) | data formatting | bytes 393216
  82.9 0.0 copy-done
  82.9 0.7 copy.11
Async XLA Ops:
  81.2 1.7 %copy-start = (f32[2,96,256]{2,1,0:T(8,128)S(1)}, f32[2,96,256]{2,1,0:T(8,128)}, u32[]{:S(2)}) copy-start(f32[2,96,256]{2,1,0:T(8,128)} %get-tuple-element.5) | copy-start | bytes 589828
